TPU v7x, 32 devices: a whole 2x2x4 slice. The times are simulated.
32 devices in a mesh: level: 2 (over y), space: 16 (over z, x, core).
Axes of the slice: x: 2, y: 2, z: 4, core: 2. Of those that a mesh axis runs over, the one named last changes fastest.
Arguments:
- start: float32 [128, 64, 128], P('space'), may hold values from -6 to 6
- source: float32 [128, 64, 128], P('space'), may hold values from -6 to 6
- past_rates: float32 [2, 10, 128, 64, 128], P('level', None, 'space'), may hold values from -6 to 6
- block_ids: int32 [2048], P('space'), may hold values from 0 to 8191, as said below
- block_bits: int32 [2048, 5], P('space'), may hold values from 0 to 1073741823
- block_drag: float32 [2048], P('space'), may hold values from 0.5 to 4
Outputs:
- mean_rates: float32 [2, 128, 64, 128], P('level', 'space')
- defects: float32 [2, 128, 64, 128], P('level', 'space')
Inputs may be any that keep to these rules, and one draw needn't show every extreme that they name: `block_ids`: entries s * 128 to (s + 1) * 128 - 1 name 128 distinct blocks z * 64 + x with z from s * 8 to (s + 1) * 8 - 1. `block_bits`: bits of a block's last word beyond cell 128 - 1 are ignored.
All inputs are finite; a program needn't handle non-finite values.
Results may differ from a plain program's by a relative error of at most 0.0002.
Values sent between devices are 32-bit elements; how exact they have to be, the bound alone decides.
A program may use at most 64 MiB of HBM per device.

v0:
```python
import jax
import jax.numpy as jnp
from jax import lax
from jax.sharding import PartitionSpec as P

STEPS = 4
NODES = 12
PAST = 10


VISCOSITY = 0.25
STEP_SIZE = 0.02


def with_halo(x, sides, width):
    for axis, dim in sides:
        size, length = (lax.axis_size(axis), x.shape[dim])
        up = [(i, (i + 1) % size) for i in range(size - 1)]
        down = [(j, i) for i, j in up]
        last = lax.slice_in_dim(x, length - width, length, axis=dim)
        first = lax.slice_in_dim(x, 0, width, axis=dim)
        before = lax.ppermute(last, axis, up)
        after = lax.ppermute(first, axis, down)
        x = jnp.concatenate([before, x, after], axis=dim)
    return x


def from_behind(x, axis, by):
    length = lax.axis_size(axis)
    pairs = [(i, i + by) for i in range(length) if 0 <= i + by < length]
    return lax.ppermute(x, axis, pairs)


def stencil_weights(count):
    points = [float(item - (count - 2)) for item in range(count)]
    result = []
    for index in range(count):
        coeffs = [1.0]
        denom = 1.0
        for other_index in range(count):
            if other_index != index:
                other = points[other_index]
                shifted = [0.0] + coeffs
                scaled = [-other * value for value in coeffs] + [0.0]
                coeffs = [first + second for first, second in zip(shifted, scaled)]
                denom = denom * (points[index] - other)
        integral = 0.0
        for power in range(len(coeffs)):
            integral = integral + coeffs[power] / (power + 1)
        result.append(integral / denom * STEP_SIZE)
    return result


def second_diff(padded):
    inner = padded[2:-2]
    total = 16.0 * (padded[1:-3] + padded[3:-1]) - (padded[:-4] + padded[4:]) - 30.0 * inner
    for axis in (1, 2):
        total = (
            total
            + 16.0 * (jnp.roll(inner, 1, axis) + jnp.roll(inner, -1, axis))
            - (jnp.roll(inner, 2, axis) + jnp.roll(inner, -2, axis))
            - 30.0 * inner
        )
    return total / 12.0


def quadrature(weights, stacked):
    return jnp.tensordot(weights, stacked, axes=1, precision=lax.Precision.HIGHEST)


def body(start, source, past_rates, block_ids, block_bits, block_drag):
    depth, rows, cols = start.shape
    weights = jnp.asarray(stencil_weights(NODES), jnp.float32)
    cells = jnp.arange(cols)
    words = jnp.take(block_bits, cells // 30, axis=1)
    coef = (jnp.right_shift(words, cells % 30) & 1).astype(jnp.float32) * block_drag[:, None]
    local_ids = block_ids - lax.axis_index("space") * (depth * rows)
    penalty = (
        jnp.zeros((depth * rows, cols), jnp.float32)
        .at[local_ids]
        .set(coef)
        .reshape(depth, rows, cols)
    )

    def rate_of(field):
        padded = with_halo(field, (("space", 0),), 2)
        return VISCOSITY * second_diff(padded) - penalty * field + source

    level = lax.axis_index("level")
    ticks = STEPS + lax.axis_size("level")
    history = past_rates[0]
    own_init = jnp.concatenate([history, jnp.zeros((STEPS + 2, depth, rows, cols), jnp.float32)])

    def record(own, node, rate):
        inside = (node >= 0) & (node <= STEPS)
        slot = jnp.where(inside, PAST + node, PAST + STEPS + 1)
        return lax.dynamic_update_index_in_dim(own, rate, slot, 0)

    def advance(state, before, node, rate, correction):
        moving = (node >= 0) & (node < STEPS)
        nxt = state + STEP_SIZE * rate + correction
        return (jnp.where(moving, nxt, state), jnp.where(moving, state, before))

    lower_hist = from_behind(history, "level", 1)
    below_init = jnp.concatenate(
        [lower_hist, jnp.zeros((STEPS + 3, depth, rows, cols), jnp.float32)]
    )

    def tick_recv(tick, carry):
        state, before, own, below = carry
        node = tick - level
        here = jnp.clip(node, 0, STEPS)
        rate = rate_of(state)
        own = record(own, node, rate)
        lower = from_behind(rate, "level", 1)
        upper = node + 1
        slot = jnp.where((upper >= 0) & (upper <= STEPS), PAST + upper, PAST + STEPS + 2)
        below = lax.dynamic_update_index_in_dim(below, lower, slot, 0)
        stencil = lax.dynamic_slice_in_dim(below, PAST + here + 2 - NODES, NODES, 0)
        correction = quadrature(weights, stencil) - STEP_SIZE * lax.dynamic_index_in_dim(
            below, PAST + here, 0, keepdims=False
        )
        state, before = advance(state, before, node, rate, correction)
        return (state, before, own, below)

    state, before, own, below = lax.fori_loop(
        0, ticks, tick_recv, (start, start, own_init, below_init)
    )
    own_sum = quadrature(weights, own[PAST + STEPS + 1 - NODES : PAST + STEPS + 1])
    defect = (state - before - own_sum) / STEP_SIZE
    mean_rate = (state - start) / (STEPS * STEP_SIZE)
    return (mean_rate[None], defect[None])


def solution(mesh):
    in_specs = (
        P("space", None, None),
        P("space", None, None),
        P("level", None, "space", None, None),
        P("space"),
        P("space", None),
        P("space"),
    )
    out_specs = (P("level", "space", None, None), P("level", "space", None, None))
    return jax.shard_map(body, mesh=mesh, in_specs=in_specs, out_specs=out_specs, check_vma=False)
```

profile of v0, /device:TPU:21, one launch (start us, length us, event | category | flops | bytes accessed | tf_op | source)
XLA Modules:
  0.0 251.4 jit_solution(13766135149282008105)
XLA Ops:
  0.6 1.3 collective-permute-start.3
  2.9 1.7 copy.28
  6.2 4.4 %concatenate.151 = f32[16,8,64,128]{3,2,1,0:T(8,128)} pad(f32[10,8,64,128]{3,2,1,0:T(8,128)} %bitcast.44, f32[]{:T(128)} %constant.228.clone.1), padding=0_6x0_0x0_0x0_0 | pad | bytes 6815748 | tf_op jit(solution)/shard_map/concatenate | solution.py:92
  10.6 1.5 scatter_custom_fusion
  12.1 48.4 %collective-permute-done.3 = f32[10,8,64,128]{3,2,1,0:T(8,128)S(1)} collective-permute-done((f32[10,8,64,128]{3,2,1,0:T(8,128)}, f32[10,8,64,128]{3,2,1,0:T(8,128)S(1)}, u32[]{:S(2)}, u32[]{:S(2)}) %collective-permute-start.3) | collective-permute-done | bytes 2621472 | tf_op jit(solution)/shard_map/ppermute | solution.py:31
  60.5 2.6 %concatenate.152 = f32[17,8,64,128]{3,2,1,0:T(8,128)} pad(f32[10,8,64,128]{3,2,1,0:T(8,128)S(1)} %collective-permute-done.3, f32[]{:T(128)} %constant.228.clone.1), padding=0_7x0_0x0_0x0_0 | pad | bytes 7077892 | tf_op jit(solution)/shard_map/concatenate | solution.py:105
  63.1 179.8 %while.24 = (s32[]{:T(128)}, f32[8,64,128]{2,1,0:T(8,128)S(1)}, f32[8,64,128]{2,1,0:T(8,128)}, f32[16,8,64,128]{3,2,1,0:T(8,128)}, f32[17,8,64,128]{3,2,1,0:T(8,...) while((s32[]{:T(128)}, f32[8,64,128]{2,1,0:T(8,128)S(1)}, ...), condition=%wide.region_2.3_spmd.clone, body=%wide.region_1.2_spmd.sunk.clone.sunk | while | flops 11862044 | bytes 25948828 | solution.py:126
  63.1 4.6 %collective-permute-start = (f32[2,64,128]{2,1,0:T(8,128)S(1)}, f32[2,64,128]{2,1,0:T(8,128)S(1)}, u32[]{:S(2)}, u32[]{:S(2)}) collective-permute-start(f32[2,64,128]{2,1,0:T(8,128)S(1)} %get-tuple-element.455), channel_id=1, source_target_pairs={{0,1},{1,2},{2,3},{3,4},{4,5},{5,6},{6,7},{7,8},{8,9},{9,10},{10,1... | collective-permute-start | bytes 196616 | tf_op jit(solution)/shard_map/while/body/eval_jaxpr/ppermute | solution.py:22
  67.6 1.9 collective-permute-start.1
  71.0 2.2 collective-permute-done.1
  73.2 2.4 bitcast_dynamic-update-slice_fusion.4
  76.9 8.7 %collective-permute-done.2 = f32[8,64,128]{2,1,0:T(8,128)S(1)} collective-permute-done((f32[8,64,128]{2,1,0:T(8,128)S(1)}, f32[8,64,128]{2,1,0:T(8,128)S(1)}, u32[]{:S(2)}, u32[]{:S(2)}) %collective-permute-start.2) | collective-permute-done | bytes 262176 | tf_op jit(solution)/shard_map/while/body/eval_jaxpr/ppermute | solution.py:31
  86.3 2.2 constant_dynamic-slice_fusion.2
  88.5 5.4 %fusion.58 = f32[1,8,64,128]{3,0,2,1:T(1,128)S(1)} fusion(f32[12,1,1,1]{0,1,3,2:T(1,128)S(1)} %get-tuple-element.510, f32[12,8,64,128]{3,2,1,0:T(8,128)S(1)} %constant_dynamic-slice_fusion.2), kind=kOutput, calls=%fused_computation.2.clone.1 | convolution fusion | flops 9437184 | bytes 3407920 | tf_op jit(solution)/shard_map/while/body/eval_jaxpr/dot_general | solution.py:68
  95.8 1.9 collective-permute-start
  97.7 2.5 %collective-permute-start.1 = (f32[2,64,128]{2,1,0:T(8,128)S(1)}, f32[2,64,128]{2,1,0:T(8,128)S(1)}, u32[]{:S(2)}, u32[]{:S(2)}) collective-permute-start(f32[2,64,128]{2,1,0:T(8,128)S(1)} %get-tuple-element.457), channel_id=1, source_target_pairs={{1,0},{2,1},{3,2},{4,3},{5,4},{6,5},{7,6},{8,7},{9,8},{10,9},{11,1... | collective-permute-start | bytes 196616 | tf_op jit(solution)/shard_map/while/body/eval_jaxpr/ppermute | solution.py:23
  101.7 1.6 collective-permute-done.1
  103.3 2.3 bitcast_dynamic-update-slice_fusion.4
  107.0 6.9 %collective-permute-done.2 = f32[8,64,128]{2,1,0:T(8,128)S(1)} collective-permute-done((f32[8,64,128]{2,1,0:T(8,128)S(1)}, f32[8,64,128]{2,1,0:T(8,128)S(1)}, u32[]{:S(2)}, u32[]{:S(2)}) %collective-permute-start.2) | collective-permute-done | bytes 262176 | tf_op jit(solution)/shard_map/while/body/eval_jaxpr/ppermute | solution.py:31
  114.6 2.2 constant_dynamic-slice_fusion.2
  116.8 5.4 %fusion.58 = f32[1,8,64,128]{3,0,2,1:T(1,128)S(1)} fusion(f32[12,1,1,1]{0,1,3,2:T(1,128)S(1)} %get-tuple-element.510, f32[12,8,64,128]{3,2,1,0:T(8,128)S(1)} %constant_dynamic-slice_fusion.2), kind=kOutput, calls=%fused_computation.2.clone.1 | convolution fusion | flops 9437184 | bytes 3407920 | tf_op jit(solution)/shard_map/while/body/eval_jaxpr/dot_general | solution.py:68
  124.1 2.4 collective-permute-start
  126.5 3.8 %collective-permute-start.1 = (f32[2,64,128]{2,1,0:T(8,128)S(1)}, f32[2,64,128]{2,1,0:T(8,128)S(1)}, u32[]{:S(2)}, u32[]{:S(2)}) collective-permute-start(f32[2,64,128]{2,1,0:T(8,128)S(1)} %get-tuple-element.457), channel_id=1, source_target_pairs={{1,0},{2,1},{3,2},{4,3},{5,4},{6,5},{7,6},{8,7},{9,8},{10,9},{11,1... | collective-permute-start | bytes 196616 | tf_op jit(solution)/shard_map/while/body/eval_jaxpr/ppermute | solution.py:23
  133.0 2.3 bitcast_dynamic-update-slice_fusion.4
  136.7 6.5 %collective-permute-done.2 = f32[8,64,128]{2,1,0:T(8,128)S(1)} collective-permute-done((f32[8,64,128]{2,1,0:T(8,128)S(1)}, f32[8,64,128]{2,1,0:T(8,128)S(1)}, u32[]{:S(2)}, u32[]{:S(2)}) %collective-permute-start.2) | collective-permute-done | bytes 262176 | tf_op jit(solution)/shard_map/while/body/eval_jaxpr/ppermute | solution.py:31
  143.9 2.2 constant_dynamic-slice_fusion.2
  146.1 5.4 %fusion.58 = f32[1,8,64,128]{3,0,2,1:T(1,128)S(1)} fusion(f32[12,1,1,1]{0,1,3,2:T(1,128)S(1)} %get-tuple-element.510, f32[12,8,64,128]{3,2,1,0:T(8,128)S(1)} %constant_dynamic-slice_fusion.2), kind=kOutput, calls=%fused_computation.2.clone.1 | convolution fusion | flops 9437184 | bytes 3407920 | tf_op jit(solution)/shard_map/while/body/eval_jaxpr/dot_general | solution.py:68
  153.4 3.1 %collective-permute-start = (f32[2,64,128]{2,1,0:T(8,128)S(1)}, f32[2,64,128]{2,1,0:T(8,128)S(1)}, u32[]{:S(2)}, u32[]{:S(2)}) collective-permute-start(f32[2,64,128]{2,1,0:T(8,128)S(1)} %get-tuple-element.455), channel_id=1, source_target_pairs={{0,1},{1,2},{2,3},{3,4},{4,5},{5,6},{6,7},{7,8},{8,9},{9,10},{10,1... | collective-permute-start | bytes 196616 | tf_op jit(solution)/shard_map/while/body/eval_jaxpr/ppermute | solution.py:22
  156.5 3.5 %collective-permute-start.1 = (f32[2,64,128]{2,1,0:T(8,128)S(1)}, f32[2,64,128]{2,1,0:T(8,128)S(1)}, u32[]{:S(2)}, u32[]{:S(2)}) collective-permute-start(f32[2,64,128]{2,1,0:T(8,128)S(1)} %get-tuple-element.457), channel_id=1, source_target_pairs={{1,0},{2,1},{3,2},{4,3},{5,4},{6,5},{7,6},{8,7},{9,8},{10,9},{11,1... | collective-permute-start | bytes 196616 | tf_op jit(solution)/shard_map/while/body/eval_jaxpr/ppermute | solution.py:23
  161.4 1.6 collective-permute-done.1
  163.1 2.3 bitcast_dynamic-update-slice_fusion.4
  166.7 6.9 %collective-permute-done.2 = f32[8,64,128]{2,1,0:T(8,128)S(1)} collective-permute-done((f32[8,64,128]{2,1,0:T(8,128)S(1)}, f32[8,64,128]{2,1,0:T(8,128)S(1)}, u32[]{:S(2)}, u32[]{:S(2)}) %collective-permute-start.2) | collective-permute-done | bytes 262176 | tf_op jit(solution)/shard_map/while/body/eval_jaxpr/ppermute | solution.py:31
  174.3 2.2 constant_dynamic-slice_fusion.2
  176.5 5.4 %fusion.58 = f32[1,8,64,128]{3,0,2,1:T(1,128)S(1)} fusion(f32[12,1,1,1]{0,1,3,2:T(1,128)S(1)} %get-tuple-element.510, f32[12,8,64,128]{3,2,1,0:T(8,128)S(1)} %constant_dynamic-slice_fusion.2), kind=kOutput, calls=%fused_computation.2.clone.1 | convolution fusion | flops 9437184 | bytes 3407920 | tf_op jit(solution)/shard_map/while/body/eval_jaxpr/dot_general | solution.py:68
  183.8 1.9 collective-permute-start
  185.8 4.3 %collective-permute-start.1 = (f32[2,64,128]{2,1,0:T(8,128)S(1)}, f32[2,64,128]{2,1,0:T(8,128)S(1)}, u32[]{:S(2)}, u32[]{:S(2)}) collective-permute-start(f32[2,64,128]{2,1,0:T(8,128)S(1)} %get-tuple-element.457), channel_id=1, source_target_pairs={{1,0},{2,1},{3,2},{4,3},{5,4},{6,5},{7,6},{8,7},{9,8},{10,9},{11,1... | collective-permute-start | bytes 196616 | tf_op jit(solution)/shard_map/while/body/eval_jaxpr/ppermute | solution.py:23
  192.7 2.4 bitcast_dynamic-update-slice_fusion.4
  196.5 6.5 %collective-permute-done.2 = f32[8,64,128]{2,1,0:T(8,128)S(1)} collective-permute-done((f32[8,64,128]{2,1,0:T(8,128)S(1)}, f32[8,64,128]{2,1,0:T(8,128)S(1)}, u32[]{:S(2)}, u32[]{:S(2)}) %collective-permute-start.2) | collective-permute-done | bytes 262176 | tf_op jit(solution)/shard_map/while/body/eval_jaxpr/ppermute | solution.py:31
  203.7 2.2 constant_dynamic-slice_fusion.2
  205.8 5.4 %fusion.58 = f32[1,8,64,128]{3,0,2,1:T(1,128)S(1)} fusion(f32[12,1,1,1]{0,1,3,2:T(1,128)S(1)} %get-tuple-element.510, f32[12,8,64,128]{3,2,1,0:T(8,128)S(1)} %constant_dynamic-slice_fusion.2), kind=kOutput, calls=%fused_computation.2.clone.1 | convolution fusion | flops 9437184 | bytes 3407920 | tf_op jit(solution)/shard_map/while/body/eval_jaxpr/dot_general | solution.py:68
  213.2 2.5 collective-permute-start
  215.6 4.1 %collective-permute-start.1 = (f32[2,64,128]{2,1,0:T(8,128)S(1)}, f32[2,64,128]{2,1,0:T(8,128)S(1)}, u32[]{:S(2)}, u32[]{:S(2)}) collective-permute-start(f32[2,64,128]{2,1,0:T(8,128)S(1)} %get-tuple-element.457), channel_id=1, source_target_pairs={{1,0},{2,1},{3,2},{4,3},{5,4},{6,5},{7,6},{8,7},{9,8},{10,9},{11,1... | collective-permute-start | bytes 196616 | tf_op jit(solution)/shard_map/while/body/eval_jaxpr/ppermute | solution.py:23
  222.5 2.4 bitcast_dynamic-update-slice_fusion.4
  226.1 6.5 %collective-permute-done.2 = f32[8,64,128]{2,1,0:T(8,128)S(1)} collective-permute-done((f32[8,64,128]{2,1,0:T(8,128)S(1)}, f32[8,64,128]{2,1,0:T(8,128)S(1)}, u32[]{:S(2)}, u32[]{:S(2)}) %collective-permute-start.2) | collective-permute-done | bytes 262176 | tf_op jit(solution)/shard_map/while/body/eval_jaxpr/ppermute | solution.py:31
  233.4 2.2 constant_dynamic-slice_fusion.2
  235.5 5.4 %fusion.58 = f32[1,8,64,128]{3,0,2,1:T(1,128)S(1)} fusion(f32[12,1,1,1]{0,1,3,2:T(1,128)S(1)} %get-tuple-element.510, f32[12,8,64,128]{3,2,1,0:T(8,128)S(1)} %constant_dynamic-slice_fusion.2), kind=kOutput, calls=%fused_computation.2.clone.1 | convolution fusion | flops 9437184 | bytes 3407920 | tf_op jit(solution)/shard_map/while/body/eval_jaxpr/dot_general | solution.py:68
  242.9 2.2 slice.309
  245.0 5.4 %fusion.18 = f32[1,8,64,128]{3,0,2,1:T(1,128)S(1)} fusion(f32[12,1,1,1]{0,1,3,2:T(1,128)S(1)} %get-tuple-element.525, f32[12,8,64,128]{3,2,1,0:T(8,128)S(1)} %slice.309), kind=kOutput, calls=%fused_computation.35 | convolution fusion | flops 9437184 | bytes 3407920 | tf_op jit(solution)/shard_map/dot_general | solution.py:68
  (143 shorter events, 38.6 us)
Async XLA Ops:
  0.6 4.0 %copy-start = (s32[128,5]{0,1:T(8,128)S(1)}, s32[128,5]{0,1:T(8,128)}, u32[]{:S(2)}) copy-start(s32[128,5]{0,1:T(8,128)} %param.13) | copy-start | bytes 7684
  0.6 59.8 %collective-permute-start.3 = (f32[10,8,64,128]{3,2,1,0:T(8,128)}, f32[10,8,64,128]{3,2,1,0:T(8,128)S(1)}, u32[]{:S(2)}, u32[]{:S(2)}) collective-permute-start(f32[10,8,64,128]{3,2,1,0:T(8,128)} %bitcast.43), channel_id=1, source_target_pairs={{0,16},{1,17},{2,18},{3,19},{4,20},{5,21},{6,22},{7,23},{8,24},{9,... | collective-permute-start | bytes 7864328 | tf_op jit(solution)/shard_map/ppermute | solution.py:31
  2.9 7.7 %copy-start.6 = (s32[128]{0:T(128)S(1)}, s32[128]{0:T(128)}, u32[]{:S(2)}) copy-start(s32[128]{0:T(128)} %param.12) | copy-start | bytes 1540
  10.6 52.5 %copy-start.5 = (f32[12,1,1,1]{0,1,3,2:T(1,128)S(1)}, f32[12,1,1,1]{0,1,3,2:T(1,128)}, u32[]{:S(2)}) copy-start(f32[12,1,1,1]{0,1,3,2:T(1,128)} %constant.249) | copy-start | bytes 148
  63.1 7.8 %collective-permute-start = (f32[2,64,128]{2,1,0:T(8,128)S(1)}, f32[2,64,128]{2,1,0:T(8,128)S(1)}, u32[]{:S(2)}, u32[]{:S(2)}) collective-permute-start(f32[2,64,128]{2,1,0:T(8,128)S(1)} %get-tuple-element.455), channel_id=1, source_target_pairs={{0,1},{1,2},{2,3},{3,4},{4,5},{5,6},{6,7},{7,8},{8,9},{9,10},{10,1... | collective-permute-start | bytes 196616 | tf_op jit(solution)/shard_map/while/body/eval_jaxpr/ppermute | solution.py:22
  67.6 5.6 %collective-permute-start.1 = (f32[2,64,128]{2,1,0:T(8,128)S(1)}, f32[2,64,128]{2,1,0:T(8,128)S(1)}, u32[]{:S(2)}, u32[]{:S(2)}) collective-permute-start(f32[2,64,128]{2,1,0:T(8,128)S(1)} %get-tuple-element.457), channel_id=1, source_target_pairs={{1,0},{2,1},{3,2},{4,3},{5,4},{6,5},{7,6},{8,7},{9,8},{10,9},{11,1... | collective-permute-start | bytes 196616 | tf_op jit(solution)/shard_map/while/body/eval_jaxpr/ppermute | solution.py:23
  75.6 10.0 %collective-permute-start.2 = (f32[8,64,128]{2,1,0:T(8,128)S(1)}, f32[8,64,128]{2,1,0:T(8,128)S(1)}, u32[]{:S(2)}, u32[]{:S(2)}) collective-permute-start(f32[8,64,128]{2,1,0:T(8,128)S(1)} %get-tuple-element.459), channel_id=1, source_target_pairs={{0,16},{1,17},{2,18},{3,19},{4,20},{5,21},{6,22},{7,23},{8,24},{9,... | collective-permute-start | bytes 786440 | tf_op jit(solution)/shard_map/while/body/eval_jaxpr/ppermute | solution.py:31
  86.3 7.6 %copy-start.1 = (f32[8,64,128]{2,1,0:T(8,128)S(1)}, f32[8,64,128]{2,1,0:T(8,128)}, u32[]{:S(2)}) copy-start(f32[8,64,128]{2,1,0:T(8,128)} %get-tuple-element.483) | copy-start | bytes 786436 | tf_op jit(solution)/shard_map/while
  95.1 0.7 copy-start.2
  95.8 5.8 %collective-permute-start = (f32[2,64,128]{2,1,0:T(8,128)S(1)}, f32[2,64,128]{2,1,0:T(8,128)S(1)}, u32[]{:S(2)}, u32[]{:S(2)}) collective-permute-start(f32[2,64,128]{2,1,0:T(8,128)S(1)} %get-tuple-element.455), channel_id=1, source_target_pairs={{0,1},{1,2},{2,3},{3,4},{4,5},{5,6},{6,7},{7,8},{8,9},{9,10},{10,1... | collective-permute-start | bytes 196616 | tf_op jit(solution)/shard_map/while/body/eval_jaxpr/ppermute | solution.py:22
  97.7 5.6 %collective-permute-start.1 = (f32[2,64,128]{2,1,0:T(8,128)S(1)}, f32[2,64,128]{2,1,0:T(8,128)S(1)}, u32[]{:S(2)}, u32[]{:S(2)}) collective-permute-start(f32[2,64,128]{2,1,0:T(8,128)S(1)} %get-tuple-element.457), channel_id=1, source_target_pairs={{1,0},{2,1},{3,2},{4,3},{5,4},{6,5},{7,6},{8,7},{9,8},{10,9},{11,1... | collective-permute-start | bytes 196616 | tf_op jit(solution)/shard_map/while/body/eval_jaxpr/ppermute | solution.py:23
  105.7 8.2 %collective-permute-start.2 = (f32[8,64,128]{2,1,0:T(8,128)S(1)}, f32[8,64,128]{2,1,0:T(8,128)S(1)}, u32[]{:S(2)}, u32[]{:S(2)}) collective-permute-start(f32[8,64,128]{2,1,0:T(8,128)S(1)} %get-tuple-element.459), channel_id=1, source_target_pairs={{0,16},{1,17},{2,18},{3,19},{4,20},{5,21},{6,22},{7,23},{8,24},{9,... | collective-permute-start | bytes 786440 | tf_op jit(solution)/shard_map/while/body/eval_jaxpr/ppermute | solution.py:31
  114.6 7.6 %copy-start.1 = (f32[8,64,128]{2,1,0:T(8,128)S(1)}, f32[8,64,128]{2,1,0:T(8,128)}, u32[]{:S(2)}) copy-start(f32[8,64,128]{2,1,0:T(8,128)} %get-tuple-element.483) | copy-start | bytes 786436 | tf_op jit(solution)/shard_map/while
  123.4 0.7 copy-start.2
  124.1 7.6 %collective-permute-start = (f32[2,64,128]{2,1,0:T(8,128)S(1)}, f32[2,64,128]{2,1,0:T(8,128)S(1)}, u32[]{:S(2)}, u32[]{:S(2)}) collective-permute-start(f32[2,64,128]{2,1,0:T(8,128)S(1)} %get-tuple-element.455), channel_id=1, source_target_pairs={{0,1},{1,2},{2,3},{3,4},{4,5},{5,6},{6,7},{7,8},{8,9},{9,10},{10,1... | collective-permute-start | bytes 196616 | tf_op jit(solution)/shard_map/while/body/eval_jaxpr/ppermute | solution.py:22
  126.5 6.5 %collective-permute-start.1 = (f32[2,64,128]{2,1,0:T(8,128)S(1)}, f32[2,64,128]{2,1,0:T(8,128)S(1)}, u32[]{:S(2)}, u32[]{:S(2)}) collective-permute-start(f32[2,64,128]{2,1,0:T(8,128)S(1)} %get-tuple-element.457), channel_id=1, source_target_pairs={{1,0},{2,1},{3,2},{4,3},{5,4},{6,5},{7,6},{8,7},{9,8},{10,9},{11,1... | collective-permute-start | bytes 196616 | tf_op jit(solution)/shard_map/while/body/eval_jaxpr/ppermute | solution.py:23
  135.4 7.9 %collective-permute-start.2 = (f32[8,64,128]{2,1,0:T(8,128)S(1)}, f32[8,64,128]{2,1,0:T(8,128)S(1)}, u32[]{:S(2)}, u32[]{:S(2)}) collective-permute-start(f32[8,64,128]{2,1,0:T(8,128)S(1)} %get-tuple-element.459), channel_id=1, source_target_pairs={{0,16},{1,17},{2,18},{3,19},{4,20},{5,21},{6,22},{7,23},{8,24},{9,... | collective-permute-start | bytes 786440 | tf_op jit(solution)/shard_map/while/body/eval_jaxpr/ppermute | solution.py:31
  143.9 7.6 %copy-start.1 = (f32[8,64,128]{2,1,0:T(8,128)S(1)}, f32[8,64,128]{2,1,0:T(8,128)}, u32[]{:S(2)}) copy-start(f32[8,64,128]{2,1,0:T(8,128)} %get-tuple-element.483) | copy-start | bytes 786436 | tf_op jit(solution)/shard_map/while
  152.7 0.7 copy-start.2
  153.4 7.9 %collective-permute-start = (f32[2,64,128]{2,1,0:T(8,128)S(1)}, f32[2,64,128]{2,1,0:T(8,128)S(1)}, u32[]{:S(2)}, u32[]{:S(2)}) collective-permute-start(f32[2,64,128]{2,1,0:T(8,128)S(1)} %get-tuple-element.455), channel_id=1, source_target_pairs={{0,1},{1,2},{2,3},{3,4},{4,5},{5,6},{6,7},{7,8},{8,9},{9,10},{10,1... | collective-permute-start | bytes 196616 | tf_op jit(solution)/shard_map/while/body/eval_jaxpr/ppermute | solution.py:22
  156.5 6.5 %collective-permute-start.1 = (f32[2,64,128]{2,1,0:T(8,128)S(1)}, f32[2,64,128]{2,1,0:T(8,128)S(1)}, u32[]{:S(2)}, u32[]{:S(2)}) collective-permute-start(f32[2,64,128]{2,1,0:T(8,128)S(1)} %get-tuple-element.457), channel_id=1, source_target_pairs={{1,0},{2,1},{3,2},{4,3},{5,4},{6,5},{7,6},{8,7},{9,8},{10,9},{11,1... | collective-permute-start | bytes 196616 | tf_op jit(solution)/shard_map/while/body/eval_jaxpr/ppermute | solution.py:23
  165.4 8.2 %collective-permute-start.2 = (f32[8,64,128]{2,1,0:T(8,128)S(1)}, f32[8,64,128]{2,1,0:T(8,128)S(1)}, u32[]{:S(2)}, u32[]{:S(2)}) collective-permute-start(f32[8,64,128]{2,1,0:T(8,128)S(1)} %get-tuple-element.459), channel_id=1, source_target_pairs={{0,16},{1,17},{2,18},{3,19},{4,20},{5,21},{6,22},{7,23},{8,24},{9,... | collective-permute-start | bytes 786440 | tf_op jit(solution)/shard_map/while/body/eval_jaxpr/ppermute | solution.py:31
  174.3 7.6 %copy-start.1 = (f32[8,64,128]{2,1,0:T(8,128)S(1)}, f32[8,64,128]{2,1,0:T(8,128)}, u32[]{:S(2)}) copy-start(f32[8,64,128]{2,1,0:T(8,128)} %get-tuple-element.483) | copy-start | bytes 786436 | tf_op jit(solution)/shard_map/while
  183.1 0.7 copy-start.2
  183.8 7.6 %collective-permute-start = (f32[2,64,128]{2,1,0:T(8,128)S(1)}, f32[2,64,128]{2,1,0:T(8,128)S(1)}, u32[]{:S(2)}, u32[]{:S(2)}) collective-permute-start(f32[2,64,128]{2,1,0:T(8,128)S(1)} %get-tuple-element.455), channel_id=1, source_target_pairs={{0,1},{1,2},{2,3},{3,4},{4,5},{5,6},{6,7},{7,8},{8,9},{9,10},{10,1... | collective-permute-start | bytes 196616 | tf_op jit(solution)/shard_map/while/body/eval_jaxpr/ppermute | solution.py:22
  185.8 7.0 %collective-permute-start.1 = (f32[2,64,128]{2,1,0:T(8,128)S(1)}, f32[2,64,128]{2,1,0:T(8,128)S(1)}, u32[]{:S(2)}, u32[]{:S(2)}) collective-permute-start(f32[2,64,128]{2,1,0:T(8,128)S(1)} %get-tuple-element.457), channel_id=1, source_target_pairs={{1,0},{2,1},{3,2},{4,3},{5,4},{6,5},{7,6},{8,7},{9,8},{10,9},{11,1... | collective-permute-start | bytes 196616 | tf_op jit(solution)/shard_map/while/body/eval_jaxpr/ppermute | solution.py:23
  195.1 7.8 %collective-permute-start.2 = (f32[8,64,128]{2,1,0:T(8,128)S(1)}, f32[8,64,128]{2,1,0:T(8,128)S(1)}, u32[]{:S(2)}, u32[]{:S(2)}) collective-permute-start(f32[8,64,128]{2,1,0:T(8,128)S(1)} %get-tuple-element.459), channel_id=1, source_target_pairs={{0,16},{1,17},{2,18},{3,19},{4,20},{5,21},{6,22},{7,23},{8,24},{9,... | collective-permute-start | bytes 786440 | tf_op jit(solution)/shard_map/while/body/eval_jaxpr/ppermute | solution.py:31
  203.7 7.6 %copy-start.1 = (f32[8,64,128]{2,1,0:T(8,128)S(1)}, f32[8,64,128]{2,1,0:T(8,128)}, u32[]{:S(2)}) copy-start(f32[8,64,128]{2,1,0:T(8,128)} %get-tuple-element.483) | copy-start | bytes 786436 | tf_op jit(solution)/shard_map/while
  212.4 0.7 copy-start.2
  213.2 8.0 %collective-permute-start = (f32[2,64,128]{2,1,0:T(8,128)S(1)}, f32[2,64,128]{2,1,0:T(8,128)S(1)}, u32[]{:S(2)}, u32[]{:S(2)}) collective-permute-start(f32[2,64,128]{2,1,0:T(8,128)S(1)} %get-tuple-element.455), channel_id=1, source_target_pairs={{0,1},{1,2},{2,3},{3,4},{4,5},{5,6},{6,7},{7,8},{8,9},{9,10},{10,1... | collective-permute-start | bytes 196616 | tf_op jit(solution)/shard_map/while/body/eval_jaxpr/ppermute | solution.py:22
  215.6 6.8 %collective-permute-start.1 = (f32[2,64,128]{2,1,0:T(8,128)S(1)}, f32[2,64,128]{2,1,0:T(8,128)S(1)}, u32[]{:S(2)}, u32[]{:S(2)}) collective-permute-start(f32[2,64,128]{2,1,0:T(8,128)S(1)} %get-tuple-element.457), channel_id=1, source_target_pairs={{1,0},{2,1},{3,2},{4,3},{5,4},{6,5},{7,6},{8,7},{9,8},{10,9},{11,1... | collective-permute-start | bytes 196616 | tf_op jit(solution)/shard_map/while/body/eval_jaxpr/ppermute | solution.py:23
  224.8 7.8 %collective-permute-start.2 = (f32[8,64,128]{2,1,0:T(8,128)S(1)}, f32[8,64,128]{2,1,0:T(8,128)S(1)}, u32[]{:S(2)}, u32[]{:S(2)}) collective-permute-start(f32[8,64,128]{2,1,0:T(8,128)S(1)} %get-tuple-element.459), channel_id=1, source_target_pairs={{0,16},{1,17},{2,18},{3,19},{4,20},{5,21},{6,22},{7,23},{8,24},{9,... | collective-permute-start | bytes 786440 | tf_op jit(solution)/shard_map/while/body/eval_jaxpr/ppermute | solution.py:31
  233.4 7.6 %copy-start.1 = (f32[8,64,128]{2,1,0:T(8,128)S(1)}, f32[8,64,128]{2,1,0:T(8,128)}, u32[]{:S(2)}) copy-start(f32[8,64,128]{2,1,0:T(8,128)} %get-tuple-element.483) | copy-start | bytes 786436 | tf_op jit(solution)/shard_map/while
  242.2 0.7 copy-start.2
  242.9 7.6 %copy-start.3 = (f32[8,64,128]{2,1,0:T(8,128)S(1)}, f32[8,64,128]{2,1,0:T(8,128)}, u32[]{:S(2)}) copy-start(f32[8,64,128]{2,1,0:T(8,128)} %get-tuple-element.295) | copy-start | bytes 786436
  242.9 7.6 %copy-start.4 = (f32[8,64,128]{2,1,0:T(8,128)S(1)}, f32[8,64,128]{2,1,0:T(8,128)}, u32[]{:S(2)}) copy-start(f32[8,64,128]{2,1,0:T(8,128)} %param.9) | copy-start | bytes 786436
where the time goes:
time: 255 us; the launch traced here: 251 us
  waiting for transfers between devices  99.7 us (39%)
  starting transfers between devices  45.5 us (18%)
  local copies, waits for them, and re-layouts  43.6 us (17%)
  matrix products  38 us (15%)
  other arithmetic  22.9 us (9%)
    ppermute x7, waiting for transfers between devices, from_behind(): return lax.ppermute(x, axis, pairs)  90.4 us
    dot_general x7, matrix products, quadrature(): jnp.tensordot(weights, stacked, axes=1, precision=lax.Precision.HIGHEST)  38 us
    ppermute x6, starting transfers between devices, with_halo(): after = lax.ppermute(first, axis, down)  20.2 us
    ppermute x6, starting transfers between devices, with_halo(): before = lax.ppermute(last, axis, up)  16.4 us
    dynamic_update_slice x6, other arithmetic, record(): return lax.dynamic_update_index_in_dim(own, rate, slot, 0)  14.1 us
    dynamic_slice x6, local copies, waits for them, and re-layouts, tick_recv(): stencil = lax.dynamic_slice_in_dim(below, PAST + here + 2 - NODES, NODES, 0)  12.9 us
    ppermute x6, waiting for transfers between devices, with_halo(): after = lax.ppermute(first, axis, down)  9.29 us
    ppermute x7, starting transfers between devices, from_behind(): return lax.ppermute(x, axis, pairs)  8.97 us
  transfers between devices with their start and end apart: 19, of which 13 were waited for; matrix products, arithmetic and copies ran while one was open for 7% of the time, Pallas kernels for 0%

commit v1 on v0

--- a/solution.py
+++ b/solution.py
@@ -1,6 +1,10 @@
+import functools
+
 import jax
 import jax.numpy as jnp
 from jax import lax
+from jax.experimental import pallas as pl
+from jax.experimental.pallas import tpu as pltpu
 from jax.sharding import PartitionSpec as P
 
 STEPS = 4
@@ -132,6 +136,415 @@
     return (mean_rate[None], defect[None])
 
 
+def kernel(
+    n,
+    weights,
+    start_ref,
+    source_ref,
+    past_ref,
+    ids_ref,
+    bits_ref,
+    drag_ref,
+    mean_ref,
+    defect_ref,
+    u_buf,
+    g_buf,
+    rates,
+    past,
+    sums,
+    source,
+    drag,
+    acc,
+    moved,
+    result,
+    ids,
+    bits,
+    scale,
+    halo_send,
+    halo_recv,
+    move_send,
+    move_recv,
+    load_sem,
+    out_sem,
+):
+    w = weights
+    h = STEP_SIZE
+    depth, rows, cols = source.shape
+    level = lax.axis_index("level")
+    s = lax.axis_index("space")
+    lower, upper = jnp.maximum(s - 1, 0), jnp.minimum(s + 1, n - 1)
+    has_lower, has_upper = s > 0, s < n - 1
+    fields = (u_buf, g_buf)
+
+    loads = [
+        pltpu.make_async_copy(past_ref.at[0], past, load_sem.at[0]),
+        pltpu.make_async_copy(start_ref, u_buf.at[0, pl.ds(2, depth)], load_sem.at[1]),
+        pltpu.make_async_copy(source_ref, source, load_sem.at[2]),
+        pltpu.make_async_copy(ids_ref, ids, load_sem.at[3]),
+        pltpu.make_async_copy(bits_ref, bits, load_sem.at[4]),
+        pltpu.make_async_copy(drag_ref, scale, load_sem.at[5]),
+    ]
+    for load in loads:
+        load.start()
+
+    barrier = pltpu.get_barrier_semaphore()
+
+    def greet(where):
+        pl.semaphore_signal(
+            barrier, inc=1, device_id=where, device_id_type=pl.DeviceIdType.MESH
+        )
+
+    greet({"level": 1 - level})
+
+    @pl.when(has_lower)
+    def _():
+        greet({"space": lower})
+
+    @pl.when(has_upper)
+    def _():
+        greet({"space": upper})
+
+    zero = jnp.zeros((2, rows, cols), jnp.float32)
+
+    @pl.when(s == 0)
+    def _():
+        for field in fields:
+            for q in range(field.shape[0]):
+                field[q, 0:2] = zero
+
+    @pl.when(s == n - 1)
+    def _():
+        for field in fields:
+            for q in range(field.shape[0]):
+                field[q, depth + 2 : depth + 4] = zero
+
+    peers = 1 + has_lower.astype(jnp.int32) + has_upper.astype(jnp.int32)
+    pl.semaphore_wait(barrier, peers)
+
+    def halo(f, q):
+        buf = fields[f]
+        down = pltpu.make_async_remote_copy(
+            src_ref=buf.at[q, pl.ds(2, 2)],
+            dst_ref=buf.at[q, pl.ds(depth + 2, 2)],
+            send_sem=halo_send.at[f, q, 0],
+            recv_sem=halo_recv.at[f, q, 0],
+            device_id={"space": lower},
+            device_id_type=pl.DeviceIdType.MESH,
+        )
+        up = pltpu.make_async_remote_copy(
+            src_ref=buf.at[q, pl.ds(depth, 2)],
+            dst_ref=buf.at[q, pl.ds(0, 2)],
+            send_sem=halo_send.at[f, q, 1],
+            recv_sem=halo_recv.at[f, q, 1],
+            device_id={"space": upper},
+            device_id_type=pl.DeviceIdType.MESH,
+        )
+        return down, up
+
+    def send(f, q):
+        down, up = halo(f, q)
+        pl.when(has_lower)(down.start)
+        pl.when(has_upper)(up.start)
+
+    def recv(f, q):
+        down, up = halo(f, q)
+        pl.when(has_upper)(down.wait_recv)
+        pl.when(has_lower)(up.wait_recv)
+
+    def drain(f, q):
+        down, up = halo(f, q)
+        pl.when(has_lower)(down.wait_send)
+        pl.when(has_upper)(up.wait_send)
+
+    def edge(step):
+        @pl.loop(0, 4)
+        def _(i):
+            step(i + (i // 2) * (depth - 4))
+
+    def inner(step):
+        @pl.loop(2, depth - 2)
+        def _(z):
+            step(z)
+
+    def every(step):
+        @pl.loop(0, depth)
+        def _(z):
+            step(z)
+
+    near_scale = VISCOSITY * 16.0 / 12.0
+    far_scale = VISCOSITY / 12.0
+
+    def turn(x, by, axis):
+        return pltpu.roll(x, by % x.shape[axis], axis)
+
+    def applied(buf, q, z):
+        x = buf[q, z + 2]
+        near = buf[q, z + 1] + buf[q, z + 3]
+        far = buf[q, z] + buf[q, z + 4]
+        for axis in (0, 1):
+            near = near + (turn(x, 1, axis) + turn(x, -1, axis))
+            far = far + (turn(x, 2, axis) + turn(x, -2, axis))
+        return near_scale * near - far_scale * far - drag[z] * x
+
+    def past_sum(z, shift):
+        total = w[0] * past[shift, z]
+        for i in range(shift + 1, PAST):
+            total = total + w[i - shift] * past[i, z]
+        return total
+
+    def make_drag():
+        for load in loads[3:]:
+            load.wait()
+        words = bits[...]
+        cell = lax.broadcasted_iota(jnp.int32, (cols, words.shape[1]), 0)
+        word = jnp.broadcast_to(words[0:1], cell.shape)
+        low = jnp.zeros_like(cell)
+        for i in range(1, words.shape[0]):
+            word = jnp.where(cell >= 30 * i, words[i : i + 1], word)
+            low = jnp.where(cell >= 30 * i, 30 * i, low)
+        mask = jnp.right_shift(word, cell - low) & 1
+        value = mask.astype(jnp.float32) * scale[...]
+        parts = []
+        for _ in range(3):
+            part = value.astype(jnp.bfloat16)
+            parts.append(part)
+            value = value - part.astype(jnp.float32)
+        local = ids[...] - s * (depth * rows)
+        row = lax.broadcasted_iota(jnp.int32, (rows, local.shape[1]), 0)
+
+        def place(z):
+            pick = jnp.where(row + z * rows == local, 1.0, 0.0).astype(jnp.bfloat16)
+            total = 90.0 * VISCOSITY / 12.0
+            for part in reversed(parts):
+                total = total + lax.dot_general(
+                    pick,
+                    part,
+                    (((1,), (1,)), ((), ())),
+                    preferred_element_type=jnp.float32,
+                )
+            drag[z] = total
+
+        every(place)
+
+    chunks = depth // 2
+
+    def move(i, c):
+        return pltpu.make_async_remote_copy(
+            src_ref=moved.at[i, pl.ds(2 * c, 2)],
+            dst_ref=moved.at[i, pl.ds(2 * c, 2)],
+            send_sem=move_send.at[i, c],
+            recv_sem=move_recv.at[i, c],
+            device_id={"level": 1 - level},
+            device_id_type=pl.DeviceIdType.MESH,
+        )
+
+    def store(i, c):
+        target = (mean_ref, defect_ref)[i]
+        return pltpu.make_async_copy(
+            result.at[i, pl.ds(2 * c, 2)], target.at[0, pl.ds(2 * c, 2)], out_sem.at[i, c]
+        )
+
+    order = [0, chunks - 1] + list(range(1, chunks - 1))
+
+    def step_u(q, z):
+        rate = applied(u_buf, q, z) + source[z]
+        if q < STEPS:
+            u_buf[q + 1, z + 2] = u_buf[q, z + 2] + h * rate
+        return rate
+
+    @pl.when(level == 0)
+    def _():
+        def first(z):
+            g_buf[0, z + 2] = past_sum(z, 0)
+
+        loads[0].wait()
+        edge(first)
+        send(1, 0)
+        loads[1].wait()
+        send(0, 0)
+        inner(first)
+
+        def later(z):
+            for i in range(3):
+                sums[i, z] = past_sum(z, i + 1)
+
+        every(later)
+        make_drag()
+        loads[2].wait()
+
+        def step_v(q, z):
+            a = applied(g_buf, q, z)
+            if q == 3:
+                moved[1, z] = (acc[1, z] - w[11] * a) * (1.0 / h)
+                return
+            extra = sums[q, z]
+            v = g_buf[q, z + 2] + (h * a + extra)
+            g_buf[q + 1, z + 2] = v
+            if q == 0:
+                acc[1, z] = -w[8] * a
+            if q == 1:
+                acc[1, z] = acc[1, z] - w[9] * a
+            if q == 2:
+                acc[1, z] = acc[1, z] + (extra + (h - w[10]) * a)
+                moved[0, z] = v * (1.0 / (STEPS * h))
+
+        def step_own(q, z):
+            rate = step_u(q, z)
+            if q == 0:
+                rates[0, z] = rate
+                acc[0, z] = -sums[2, z] - w[7] * rate
+            elif q < 4:
+                rates[0, z] = rates[0, z] + rate
+                c = w[7 + q] if q < 3 else w[10] - h
+                acc[0, z] = acc[0, z] - c * rate
+            if q == 3:
+                result[0, z] = rates[0, z] * (1.0 / STEPS)
+            if q == 4:
+                result[1, z] = (acc[0, z] - w[11] * rate) * (1.0 / h)
+
+        for q in range(5):
+            if q < 4:
+                recv(1, q)
+                edge(functools.partial(step_v, q))
+                if q < 3:
+                    send(1, q + 1)
+                if q == 2:
+                    for c in order[:2]:
+                        move(0, c).start()
+                if q == 3:
+                    for c in order[:2]:
+                        move(1, c).start()
+                inner(functools.partial(step_v, q))
+                if q == 2:
+                    for c in order[2:]:
+                        move(0, c).start()
+                if q == 3:
+                    for c in order[2:]:
+                        move(1, c).start()
+            recv(0, q)
+            edge(functools.partial(step_own, q))
+            if q < 4:
+                send(0, q + 1)
+            inner(functools.partial(step_own, q))
+            if q == 3:
+                for c in order:
+                    store(0, c).start()
+        for c in order:
+            store(1, c).start()
+        for i in range(2):
+            for c in order:
+                move(i, c).wait_send()
+
+    @pl.when(level == 1)
+    def _():
+        loads[1].wait()
+        send(0, 0)
+        make_drag()
+        loads[2].wait()
+        loads[0].wait()
+
+        def step(q, z):
+            if q < 5:
+                rate = step_u(q, z)
+                rates[q, z] = rate
+            if q == 0:
+                acc[1, z] = -past_sum(z, 3) - w[7] * rate
+            if q == 1:
+                g_buf[0, z + 2] = u_buf[0, z + 2] + (w[10] * rates[0, z] + w[11] * rate)
+            if q >= 2:
+                f = applied(g_buf, q - 2, z) + source[z]
+                if q == 5:
+                    acc[1, z] = (acc[1, z] - w[11] * f) * (1.0 / h)
+                    return
+                gain = h * (f - rates[q - 1, z]) + w[11] * rate
+                for m in range(q):
+                    gain = gain + w[m + 11 - q] * rates[m, z]
+                b = g_buf[q - 2, z + 2] + gain
+                g_buf[q - 1, z + 2] = b
+                less = -w[6 + q] * f
+                if q == 4:
+                    less = less + gain
+                    acc[0, z] = (b - u_buf[0, z + 2]) * (1.0 / (STEPS * h))
+                acc[1, z] = acc[1, z] + less
+
+        for q in range(6):
+            if q < 5:
+                recv(0, q)
+            if q >= 2:
+                recv(1, q - 2)
+            edge(functools.partial(step, q))
+            if q < 4:
+                send(0, q + 1)
+            if 1 <= q < 5:
+                send(1, q - 1)
+            inner(functools.partial(step, q))
+
+        for i in range(2):
+            for c in order:
+                move(i, c).wait_recv()
+                for z in (2 * c, 2 * c + 1):
+                    result[i, z] = acc[i, z] + moved[i, z]
+                store(i, c).start()
+
+    for q in range(5):
+        drain(0, q)
+    for q in range(4):
+        drain(1, q)
+    for i in range(2):
+        for c in order:
+            store(i, c).wait()
+
+
+def fused(n, start, source, past_rates, block_ids, block_bits, block_drag):
+    shape = start.shape
+    depth, rows, cols = shape
+    padded = (depth + 4, rows, cols)
+    occupied = block_ids.shape[0]
+    words = block_bits.shape[1]
+    f32 = jnp.float32
+    anywhere = pl.BlockSpec(memory_space=pl.ANY)
+    weights = tuple(stencil_weights(NODES))
+    out = jax.ShapeDtypeStruct((1,) + shape, f32)
+    chunks = depth // 2
+    return pl.pallas_call(
+        functools.partial(kernel, n, weights),
+        out_shape=(out, out),
+        in_specs=[anywhere] * 6,
+        out_specs=(anywhere, anywhere),
+        scratch_shapes=[
+            pltpu.VMEM((5,) + padded, f32),
+            pltpu.VMEM((4,) + padded, f32),
+            pltpu.VMEM((5,) + shape, f32),
+            pltpu.VMEM((PAST,) + shape, f32),
+            pltpu.VMEM((3,) + shape, f32),
+            pltpu.VMEM(shape, f32),
+            pltpu.VMEM(shape, f32),
+            pltpu.VMEM((2,) + shape, f32),
+            pltpu.VMEM((2,) + shape, f32),
+            pltpu.VMEM((2,) + shape, f32),
+            pltpu.VMEM((1, occupied), jnp.int32),
+            pltpu.VMEM((words, occupied), jnp.int32),
+            pltpu.VMEM((1, occupied), f32),
+            pltpu.SemaphoreType.DMA((2, 5, 2)),
+            pltpu.SemaphoreType.DMA((2, 5, 2)),
+            pltpu.SemaphoreType.DMA((2, chunks)),
+            pltpu.SemaphoreType.DMA((2, chunks)),
+            pltpu.SemaphoreType.DMA((6,)),
+            pltpu.SemaphoreType.DMA((2, chunks)),
+        ],
+        compiler_params=pltpu.CompilerParams(
+            collective_id=0, has_side_effects=True, vmem_limit_bytes=60 * 2**20
+        ),
+    )(
+        start,
+        source,
+        past_rates,
+        block_ids.reshape(1, occupied),
+        block_bits.T,
+        block_drag.reshape(1, occupied),
+    )
+
+
 def solution(mesh):
     in_specs = (
         P("space", None, None),
@@ -142,4 +555,7 @@
         P("space"),
     )
     out_specs = (P("level", "space", None, None), P("level", "space", None, None))
-    return jax.shard_map(body, mesh=mesh, in_specs=in_specs, out_specs=out_specs, check_vma=False)
+    part = body
+    if mesh.shape["level"] == 2:
+        part = functools.partial(fused, mesh.shape["space"])
+    return jax.shard_map(part, mesh=mesh, in_specs=in_specs, out_specs=out_specs, check_vma=False)

time: 255 us -> 33.9 us (0.13)
  the two profiles are of different devices: /device:TPU:21 before, /device:TPU:22 now
where the time goes in v1:
time: 33.9 us; the launch traced here: 33.7 us
  Pallas kernels  29.7 us (88%)
  local copies, waits for them, and re-layouts  3.34 us (10%)
  between operations  0.64 us (2%)
    pallas_call x1, Pallas kernels, fused(): pl.pallas_call(functools.partial(kernel, n, weights), out_shape=(out, out...  29.7 us
    unnamed x2, local copies, waits for them, and re-layouts  3.34 us

profile of v1, /device:TPU:22, one launch (start us, length us, event | category | flops | bytes accessed | tf_op | source)
XLA Modules:
  0.0 33.7 jit_solution(9797879880141014643)
XLA Ops:
  0.6 29.7 %shard_map.77 = (f32[1,8,64,128]{3,2,1,0:T(8,128)}, f32[1,8,64,128]{3,2,1,0:T(8,128)}) custom-call(f32[8,64,128]{2,1,0:T(8,128)} %start_ref.1, f32[8,64,128]{2,1,0:T(8,128)} %source_ref.1, f32[1,10,8,64,128]{4,3,2,1,0:T(8,128)} %past_ref.1, s32[1,128]{1,0:T(1,128)} %bitcast.4, s32[5,128]{1,0:T(8,128)} %bitcast.3, f32[1,128]{1,0:T(1,128)} %bitcast.5), custom_call_target="tpu_custom_call" | custom-call | tf_op jit(solution)/shard_map/pallas_call | solution.py:509
  30.4 1.7 %copy.10 = f32[1,8,64,128]{3,2,1,0:T(8,128)} copy(f32[1,8,64,128]{3,2,1,0:T(8,128)} %get-tuple-element.4) | data formatting | bytes 524288
  32.0 1.7 %copy.11 = f32[1,8,64,128]{3,2,1,0:T(8,128)} copy(f32[1,8,64,128]{3,2,1,0:T(8,128)} %get-tuple-element.5) | data formatting | bytes 524288

commit v2 on v1

--- a/solution.py
+++ b/solution.py
@@ -136,6 +136,54 @@
     return (mean_rate[None], defect[None])
 
 
+SCHEDULE = (
+    ("v", 0),
+    ("s", 0),
+    ("v", 1),
+    ("z", 0),
+    ("v", 2),
+    ("z", 1),
+    ("v", 3),
+    ("z", 2),
+    ("z", 3),
+    ("z", 4),
+)
+
+
+def rate_series(w):
+    h = STEP_SIZE
+
+    def add(*terms):
+        size = max(len(series) for _, series in terms)
+        return [sum(c * series[i] for c, series in terms if i < len(series)) for i in range(size)]
+
+    results = []
+    below = None
+    for level in range(2):
+        state = [0.0]
+        own = []
+        for node in range(STEPS + 1):
+            own.append(add((1.0, [1.0]), (1.0, [0.0] + state)) if node else [1.0])
+            if node < STEPS:
+                before = state
+                state = add((1.0, state), (h, own[node]))
+                if level > 0:
+                    state = add(
+                        (1.0, state),
+                        (-h, below[node]),
+                        *((w[PAST - node + m], below[m]) for m in range(node + 2)),
+                    )
+        last = PAST + STEPS + 1 - NODES
+        defect = add(
+            (1.0, state),
+            (-1.0, before),
+            *((-w[PAST + m - last], own[m]) for m in range(STEPS + 1)),
+        )
+        results.append((state, defect))
+        below = own
+    return results
+
+
 def kernel(
     n,
     weights,
@@ -145,11 +193,9 @@
     ids_ref,
     bits_ref,
     drag_ref,
-    mean_ref,
-    defect_ref,
+    out_ref,
     u_buf,
     g_buf,
-    rates,
     past,
     sums,
     source,
@@ -157,6 +203,7 @@
     acc,
     moved,
     result,
+    share,
     ids,
     bits,
     scale,
@@ -168,6 +215,7 @@
     out_sem,
 ):
     w = weights
+    lower_coeffs, upper_coeffs = rate_series(w)
     h = STEP_SIZE
     depth, rows, cols = source.shape
     level = lax.axis_index("level")
@@ -217,9 +265,6 @@
         for field in fields:
             for q in range(field.shape[0]):
                 field[q, depth + 2 : depth + 4] = zero
-
-    peers = 1 + has_lower.astype(jnp.int32) + has_upper.astype(jnp.int32)
-    pl.semaphore_wait(barrier, peers)
 
     def halo(f, q):
         buf = fields[f]
@@ -338,30 +383,46 @@
             device_id_type=pl.DeviceIdType.MESH,
         )
 
-    def store(i, c):
-        target = (mean_ref, defect_ref)[i]
-        return pltpu.make_async_copy(
-            result.at[i, pl.ds(2 * c, 2)], target.at[0, pl.ds(2 * c, 2)], out_sem.at[i, c]
-        )
+    def store(i, c, origin=None):
+        part = pl.ds(2 * c, 2)
+        return pltpu.make_async_copy((result if origin is None else origin).at[i, part], out_ref.at[i, part], out_sem.at[i, c])
 
     order = [0, chunks - 1] + list(range(1, chunks - 1))
 
-    def step_u(q, z):
-        rate = applied(u_buf, q, z) + source[z]
-        if q < STEPS:
-            u_buf[q + 1, z + 2] = u_buf[q, z + 2] + h * rate
-        return rate
+    def first(z):
+        g_buf[0, z + 2] = past_sum(z, 0)
+
+    def step_z(coeffs, q, z):
+        rate = applied(u_buf, q, z)
+        if q == 0:
+            rate = rate + source[z]
+            acc[0, z] = coeffs[0][0] * rate
+            acc[1, z] = coeffs[1][0] * rate - (past_sum(z, 3) if coeffs is upper_coeffs else sums[2, z])
+        for i in range(2):
+            if 0 < q < len(coeffs[i]):
+                acc[i, z] = acc[i, z] + coeffs[i][q] * rate
+        if q + 1 < len(coeffs[1]):
+            u_buf[q + 1, z + 2] = rate
+
+    def round_z(coeffs, q):
+        recv(0, q)
+        edge(functools.partial(step_z, coeffs, q))
+        if q + 1 < len(coeffs[1]):
+            send(0, q + 1)
+        inner(functools.partial(step_z, coeffs, q))
 
     @pl.when(level == 0)
     def _():
-        def first(z):
-            g_buf[0, z + 2] = past_sum(z, 0)
-
         loads[0].wait()
         edge(first)
+
+    loads[1].wait()
+    peers = 1 + has_lower.astype(jnp.int32) + has_upper.astype(jnp.int32)
+    pl.semaphore_wait(barrier, peers)
+
+    @pl.when(level == 0)
+    def _():
         send(1, 0)
-        loads[1].wait()
-        send(0, 0)
         inner(first)
 
         def later(z):
@@ -375,110 +436,55 @@
         def step_v(q, z):
             a = applied(g_buf, q, z)
             if q == 3:
-                moved[1, z] = (acc[1, z] - w[11] * a) * (1.0 / h)
+                moved[1, z] = share[z] - w[11] * a
                 return
             extra = sums[q, z]
             v = g_buf[q, z + 2] + (h * a + extra)
             g_buf[q + 1, z + 2] = v
             if q == 0:
-                acc[1, z] = -w[8] * a
+                share[z] = -w[8] * a
             if q == 1:
-                acc[1, z] = acc[1, z] - w[9] * a
+                share[z] = share[z] - w[9] * a
             if q == 2:
-                acc[1, z] = acc[1, z] + (extra + (h - w[10]) * a)
-                moved[0, z] = v * (1.0 / (STEPS * h))
-
-        def step_own(q, z):
-            rate = step_u(q, z)
-            if q == 0:
-                rates[0, z] = rate
-                acc[0, z] = -sums[2, z] - w[7] * rate
-            elif q < 4:
-                rates[0, z] = rates[0, z] + rate
-                c = w[7 + q] if q < 3 else w[10] - h
-                acc[0, z] = acc[0, z] - c * rate
-            if q == 3:
-                result[0, z] = rates[0, z] * (1.0 / STEPS)
-            if q == 4:
-                result[1, z] = (acc[0, z] - w[11] * rate) * (1.0 / h)
-
-        for q in range(5):
-            if q < 4:
-                recv(1, q)
-                edge(functools.partial(step_v, q))
-                if q < 3:
-                    send(1, q + 1)
-                if q == 2:
-                    for c in order[:2]:
-                        move(0, c).start()
-                if q == 3:
-                    for c in order[:2]:
-                        move(1, c).start()
-                inner(functools.partial(step_v, q))
-                if q == 2:
-                    for c in order[2:]:
-                        move(0, c).start()
-                if q == 3:
-                    for c in order[2:]:
-                        move(1, c).start()
-            recv(0, q)
-            edge(functools.partial(step_own, q))
-            if q < 4:
-                send(0, q + 1)
-            inner(functools.partial(step_own, q))
-            if q == 3:
-                for c in order:
-                    store(0, c).start()
-        for c in order:
-            store(1, c).start()
+                share[z] = share[z] + (extra + (h - w[10]) * a)
+                moved[0, z] = v
+
+        def round_v(q):
+            recv(1, q)
+            edge(functools.partial(step_v, q))
+            if q < 3:
+                send(1, q + 1)
+            if q >= 2:
+                for c in order[:2]:
+                    move(q - 2, c).start()
+            inner(functools.partial(step_v, q))
+            if q >= 2:
+                for c in order[2:]:
+                    move(q - 2, c).start()
+
+        for task in SCHEDULE:
+            kind, q = task
+            if kind == "s":
+                send(0, 0)
+            if kind == "v":
+                round_v(q)
+            if kind == "z":
+                round_z(lower_coeffs, q)
+        for i in range(2):
+            for c in order:
+                store(i, c, acc).start()
         for i in range(2):
             for c in order:
                 move(i, c).wait_send()
 
     @pl.when(level == 1)
     def _():
-        loads[1].wait()
         send(0, 0)
         make_drag()
         loads[2].wait()
         loads[0].wait()
-
-        def step(q, z):
-            if q < 5:
-                rate = step_u(q, z)
-                rates[q, z] = rate
-            if q == 0:
-                acc[1, z] = -past_sum(z, 3) - w[7] * rate
-            if q == 1:
-                g_buf[0, z + 2] = u_buf[0, z + 2] + (w[10] * rates[0, z] + w[11] * rate)
-            if q >= 2:
-                f = applied(g_buf, q - 2, z) + source[z]
-                if q == 5:
-                    acc[1, z] = (acc[1, z] - w[11] * f) * (1.0 / h)
-                    return
-                gain = h * (f - rates[q - 1, z]) + w[11] * rate
-                for m in range(q):
-                    gain = gain + w[m + 11 - q] * rates[m, z]
-                b = g_buf[q - 2, z + 2] + gain
-                g_buf[q - 1, z + 2] = b
-                less = -w[6 + q] * f
-                if q == 4:
-                    less = less + gain
-                    acc[0, z] = (b - u_buf[0, z + 2]) * (1.0 / (STEPS * h))
-                acc[1, z] = acc[1, z] + less
-
         for q in range(6):
-            if q < 5:
-                recv(0, q)
-            if q >= 2:
-                recv(1, q - 2)
-            edge(functools.partial(step, q))
-            if q < 4:
-                send(0, q + 1)
-            if 1 <= q < 5:
-                send(1, q - 1)
-            inner(functools.partial(step, q))
-
+            round_z(upper_coeffs, q)
         for i in range(2):
             for c in order:
                 move(i, c).wait_recv()
@@ -488,8 +494,16 @@
 
     for q in range(5):
         drain(0, q)
-    for q in range(4):
-        drain(1, q)
+
+    @pl.when(level == 0)
+    def _():
+        for q in range(4):
+            drain(1, q)
+
+    @pl.when(level == 1)
+    def _():
+        drain(0, 5)
+
     for i in range(2):
         for c in order:
             store(i, c).wait()
@@ -504,17 +518,15 @@
     f32 = jnp.float32
     anywhere = pl.BlockSpec(memory_space=pl.ANY)
     weights = tuple(stencil_weights(NODES))
-    out = jax.ShapeDtypeStruct((1,) + shape, f32)
     chunks = depth // 2
-    return pl.pallas_call(
+    both = pl.pallas_call(
         functools.partial(kernel, n, weights),
-        out_shape=(out, out),
+        out_shape=jax.ShapeDtypeStruct((2,) + shape, f32),
         in_specs=[anywhere] * 6,
-        out_specs=(anywhere, anywhere),
+        out_specs=anywhere,
         scratch_shapes=[
-            pltpu.VMEM((5,) + padded, f32),
+            pltpu.VMEM((6,) + padded, f32),
             pltpu.VMEM((4,) + padded, f32),
-            pltpu.VMEM((5,) + shape, f32),
             pltpu.VMEM((PAST,) + shape, f32),
             pltpu.VMEM((3,) + shape, f32),
             pltpu.VMEM(shape, f32),
@@ -522,11 +534,12 @@
             pltpu.VMEM((2,) + shape, f32),
             pltpu.VMEM((2,) + shape, f32),
             pltpu.VMEM((2,) + shape, f32),
+            pltpu.VMEM(shape, f32),
             pltpu.VMEM((1, occupied), jnp.int32),
             pltpu.VMEM((words, occupied), jnp.int32),
             pltpu.VMEM((1, occupied), f32),
-            pltpu.SemaphoreType.DMA((2, 5, 2)),
-            pltpu.SemaphoreType.DMA((2, 5, 2)),
+            pltpu.SemaphoreType.DMA((2, 6, 2)),
+            pltpu.SemaphoreType.DMA((2, 6, 2)),
             pltpu.SemaphoreType.DMA((2, chunks)),
             pltpu.SemaphoreType.DMA((2, chunks)),
             pltpu.SemaphoreType.DMA((6,)),
@@ -543,6 +556,7 @@
         block_bits.T,
         block_drag.reshape(1, occupied),
     )
+    return both[:1] * (1.0 / (STEPS * STEP_SIZE)), both[1:] * (1.0 / STEP_SIZE)
 
 
 def solution(mesh):

time: 33.9 us -> 30.6 us (0.903)
  the two profiles are of different devices: /device:TPU:22 before, /device:TPU:17 now
where the time goes in v2:
time: 30.6 us; the launch traced here: 30.4 us
  Pallas kernels  27.9 us (91%)
  other arithmetic  1.87 us (6%)
  between operations  0.64 us (2%)
    pallas_call x1, Pallas kernels, fused(): pl.pallas_call(functools.partial(kernel, n, weights), out_shape=jax.Shape...  27.9 us
    mul x1, other arithmetic, fused(): both[1:] * (1.0 / STEP_SIZE)  1.87 us

profile of v2, /device:TPU:17, one launch (start us, length us, event | category | flops | bytes accessed | tf_op | source)
XLA Modules:
  0.0 30.4 jit_solution(10341513684383738318)
XLA Ops:
  0.6 27.9 %shard_map.77 = f32[2,8,64,128]{3,2,1,0:T(8,128)} custom-call(f32[8,64,128]{2,1,0:T(8,128)} %start_ref.1, f32[8,64,128]{2,1,0:T(8,128)} %source_ref.1, f32[1,10,8,64,128]{4,3,2,1,0:T(8,128)} %past_ref.1, s32[1,128]{1,0:T(1,128)} %bitcast.4, s32[5,128]{1,0:T(8,128)} %bitcast.3, f32[1,128]{1,0:T(1,128)} %bitcast.5), custom_call_target="tpu_custom_call" | custom-call | tf_op jit(solution)/shard_map/pallas_call | solution.py:522
  28.6 1.9 %slice_multiply_fusion = (f32[1,8,64,128]{3,2,1,0:T(8,128)}, f32[1,8,64,128]{3,2,1,0:T(8,128)}) fusion(f32[2,8,64,128]{3,2,1,0:T(8,128)} %shard_map.77), kind=kLoop, calls=%fused_computation | loop fusion | flops 131072 | bytes 1048576 | tf_op jit(solution)/shard_map/mul | solution.py:559

commit v3 on v2

--- a/solution.py
+++ b/solution.py
@@ -137,14 +137,14 @@
 
 
 SCHEDULE = (
+    ("s", 0),
     ("v", 0),
-    ("s", 0),
+    ("z", 0),
     ("v", 1),
-    ("z", 0),
+    ("z", 1),
     ("v", 2),
-    ("z", 1),
+    ("z", 2),
     ("v", 3),
-    ("z", 2),
     ("z", 3),
     ("z", 4),
 )

time: 30.6 us -> 30 us (0.980)
  the two profiles are of different devices: /device:TPU:17 before, /device:TPU:21 now
where the time goes in v3:
time: 30 us; the launch traced here: 29.8 us
  Pallas kernels  27.3 us (91%)
  other arithmetic  1.87 us (6%)
  between operations  0.64 us (2%)
    pallas_call x1, Pallas kernels, fused(): pl.pallas_call(functools.partial(kernel, n, weights), out_shape=jax.Shape...  27.3 us
    mul x1, other arithmetic, fused(): both[1:] * (1.0 / STEP_SIZE)  1.87 us

profile of v3, /device:TPU:21, one launch (start us, length us, event | category | flops | bytes accessed | tf_op | source)
XLA Modules:
  0.0 29.8 jit_solution(15698028799939056976)
XLA Ops:
  0.6 27.3 %shard_map.77 = f32[2,8,64,128]{3,2,1,0:T(8,128)} custom-call(f32[8,64,128]{2,1,0:T(8,128)} %start_ref.1, f32[8,64,128]{2,1,0:T(8,128)} %source_ref.1, f32[1,10,8,64,128]{4,3,2,1,0:T(8,128)} %past_ref.1, s32[1,128]{1,0:T(1,128)} %bitcast.4, s32[5,128]{1,0:T(8,128)} %bitcast.3, f32[1,128]{1,0:T(1,128)} %bitcast.5), custom_call_target="tpu_custom_call" | custom-call | tf_op jit(solution)/shard_map/pallas_call | solution.py:522
  27.9 1.9 %slice_multiply_fusion = (f32[1,8,64,128]{3,2,1,0:T(8,128)}, f32[1,8,64,128]{3,2,1,0:T(8,128)}) fusion(f32[2,8,64,128]{3,2,1,0:T(8,128)} %shard_map.77), kind=kLoop, calls=%fused_computation | loop fusion | flops 131072 | bytes 1048576 | tf_op jit(solution)/shard_map/mul | solution.py:559

commit v4 on v3

--- a/solution.py
+++ b/solution.py
@@ -302,12 +302,12 @@
         pl.when(has_upper)(up.wait_send)
 
     def edge(step):
-        @pl.loop(0, 4)
+        @pl.loop(0, 4, unroll=2)
         def _(i):
             step(i + (i // 2) * (depth - 4))
 
     def inner(step):
-        @pl.loop(2, depth - 2)
+        @pl.loop(2, depth - 2, unroll=2)
         def _(z):
             step(z)
 

time: 30 us -> 29.9 us (level)
  no operation moved by 1% of the time
where the time goes in v4:
time: 29.9 us; the launch traced here: 29.8 us
  Pallas kernels  27.2 us (91%)
  other arithmetic  1.87 us (6%)
  between operations  0.64 us (2%)
    pallas_call x1, Pallas kernels, fused(): pl.pallas_call(functools.partial(kernel, n, weights), out_shape=jax.Shape...  27.2 us
    mul x1, other arithmetic, fused(): both[1:] * (1.0 / STEP_SIZE)  1.87 us

profile of v4, /device:TPU:21, one launch (start us, length us, event | category | flops | bytes accessed | tf_op | source)
XLA Modules:
  0.0 29.8 jit_solution(5089267455236802803)
XLA Ops:
  0.6 27.2 %shard_map.77 = f32[2,8,64,128]{3,2,1,0:T(8,128)} custom-call(f32[8,64,128]{2,1,0:T(8,128)} %start_ref.1, f32[8,64,128]{2,1,0:T(8,128)} %source_ref.1, f32[1,10,8,64,128]{4,3,2,1,0:T(8,128)} %past_ref.1, s32[1,128]{1,0:T(1,128)} %bitcast.4, s32[5,128]{1,0:T(8,128)} %bitcast.3, f32[1,128]{1,0:T(1,128)} %bitcast.5), custom_call_target="tpu_custom_call" | custom-call | tf_op jit(solution)/shard_map/pallas_call | solution.py:522
  27.9 1.9 %slice_multiply_fusion = (f32[1,8,64,128]{3,2,1,0:T(8,128)}, f32[1,8,64,128]{3,2,1,0:T(8,128)}) fusion(f32[2,8,64,128]{3,2,1,0:T(8,128)} %shard_map.77), kind=kLoop, calls=%fused_computation | loop fusion | flops 131072 | bytes 1048576 | tf_op jit(solution)/shard_map/mul | solution.py:559
